TPU v7x, 32 devices: a whole 2x2x4 slice. The times are simulated.
32 devices in a mesh: cell: 16 (over z, y, core), tm: 2 (over x).
Axes of the slice: x: 2, y: 2, z: 4, core: 2. Of those that a mesh axis runs over, the one named last changes fastest.
Arguments:
- sketch: bfloat16 [16384, 256], P('cell', 'tm'), may hold values from -6 to 6
- tiles: bfloat16 [4, 384, 128, 128], P('tm', 'cell'), may hold values from -0.21875 to 0.21875
- row_counts: int32 [4, 16, 8], P('tm', 'cell'), may hold values from 1 to 6, 24 in all within a row
- col_index: int32 [4, 384], P('tm', 'cell'), may hold values from 0 to 127, as said below
- precision: float32 [4, 16384], P('tm', 'cell'), may hold values from 0.25 to 4
- prior: float32 [16384], P('cell'), may hold values from 0.5 to 2
Outputs:
- hessian_sketch: float32 [16384, 256], P('cell', 'tm')
Inputs may be any that keep to these rules, and one draw needn't show every extreme that they name: `col_index`: in window w, tile k (device group d = k // 24) names a parameter block from d * 8 - 4 to d * 8 + 11 within the network; in every window each group has a tile at each of the two ends of that range that lie within the network. `row_counts`: the 8 counts of one group and window add up to 24; tiles are stored row block after row block.
All inputs are finite; a program needn't handle non-finite values.
Results may differ from a plain program's by a relative error of at most 0.00087.
Values may be sent and summed in bfloat16 or wider, within the bound.
A program may use at most 64 MiB of HBM per device.

v0:
```python
import jax
import jax.numpy as jnp
from jax import lax
from jax.sharding import PartitionSpec as P

HB = 4


def padded(shard, sides, width):
    for axis, dim in sides:
        count, length = (lax.axis_size(axis), shard.shape[dim])
        up = [(i, (i + 1) % count) for i in range(count - 1)]
        down = [(j, i) for i, j in up]
        last = lax.slice_in_dim(shard, length - width, length, axis=dim)
        leading = lax.slice_in_dim(shard, 0, width, axis=dim)
        before = lax.ppermute(last, axis, up)
        after = lax.ppermute(leading, axis, down)
        shard = jnp.concatenate([before, shard, after], axis=dim)
    return shard


def from_behind(shard, axis, by):
    count = lax.axis_size(axis)
    pairs = [(i, i + by) for i in range(count) if 0 <= i + by < count]
    return lax.ppermute(shard, axis, pairs)


def local(sketch, tiles, row_counts, col_index, precision, prior):
    tile_size = tiles.shape[-1]
    windows = tiles.shape[0]
    per_device = tiles.shape[1]
    owned = sketch.shape[0] // tile_size
    row_blocks = row_counts.shape[-1]
    margin_rows = HB * tile_size
    spread = owned + 2 * HB
    first_block = lax.axis_index("cell") * owned - HB
    full_columns = lax.all_gather(sketch, "tm", axis=1, tiled=True)
    extended = padded(full_columns, (("cell", 0),), margin_rows)
    all_columns = extended.shape[1]
    ext_blocks = extended.reshape(spread, tile_size, all_columns)
    tile_pos = jnp.arange(per_device, dtype=jnp.int32)
    accum = jnp.zeros((spread, tile_size, all_columns), jnp.float32)
    for window in range(windows):
        row_ends = jnp.cumsum(row_counts[window, 0])
        tile_row = jnp.sum((tile_pos[:, None] >= row_ends[None, :]).astype(jnp.int32), axis=1)
        local_col = col_index[window] - first_block
        picked = jnp.take(ext_blocks, local_col, axis=0)
        products = jnp.einsum(
            "tij,tjk->tik", tiles[window], picked, preferred_element_type=jnp.float32
        )
        forward = jax.ops.segment_sum(
            products, tile_row, num_segments=row_blocks, indices_are_sorted=True
        )
        weighted = (forward * precision[window].reshape(row_blocks, tile_size, 1)).astype(
            jnp.bfloat16
        )
        tile_inputs = jnp.take(weighted, tile_row, axis=0)
        back = jnp.einsum(
            "tij,tik->tjk", tiles[window], tile_inputs, preferred_element_type=jnp.float32
        )
        accum = accum.at[local_col].add(back)
    accum = accum.reshape(spread * tile_size, all_columns)
    owned_rows = owned * tile_size
    from_above = from_behind(accum[:margin_rows], "cell", -1)
    from_below = from_behind(accum[margin_rows + owned_rows :], "cell", 1)
    mine = accum[margin_rows : margin_rows + owned_rows]
    mine = mine.at[:margin_rows].add(from_below)
    mine = mine.at[owned_rows - margin_rows :].add(from_above)
    curvature = lax.psum_scatter(mine, "tm", scatter_dimension=1, tiled=True)
    return prior[:, None] * sketch.astype(jnp.float32) + curvature


def solution(mesh):
    in_specs = (
        P("cell", "tm"),
        P("tm", "cell", None, None),
        P("tm", "cell", None),
        P("tm", "cell"),
        P("tm", "cell"),
        P("cell"),
    )
    out_specs = P("cell", "tm")
    return jax.shard_map(local, mesh=mesh, in_specs=in_specs, out_specs=out_specs, check_vma=False)
```

profile of v0, /device:TPU:0, one launch (start us, length us, event | category | flops | bytes accessed | tf_op | source)
XLA Modules:
  0.0 124.3 jit_solution(14001216595937213801)
XLA Ops:
  6.5 0.0 reduce-scatter.2.cloned.1.call-start
  6.5 10.3 %all_gather.3 = bf16[1024,256]{1,0:T(8,128)(2,1)S(1)} all-gather(bf16[1024,128]{1,0:T(8,128)(2,1)} %param.14), channel_id=1, replica_groups=mesh['cell'=16,'tm'=2] {'tm'}, dimensions={1}, use_global_device_ids=true | all-gather | bytes 786432 | tf_op jit(solution)/shard_map/all_gather | solution.py:37
  16.9 1.3 %collective-permute-start = (bf16[512,256]{1,0:T(8,128)(2,1)S(1)}, bf16[512,256]{1,0:T(8,128)(2,1)S(1)}, u32[]{:S(2)}, u32[]{:S(2)}) collective-permute-start(bf16[512,256]{1,0:T(8,128)(2,1)S(1)} %get-tuple-element.38), channel_id=1, source_target_pairs={{0,2},{2,4},{4,6},{6,8},{8,10},{10,12},{12,14},{14,16},{16,18},{18... | collective-permute-start | bytes 786440 | tf_op jit(solution)/shard_map/ppermute | solution.py:16
  18.2 1.3 %collective-permute-start.1 = (bf16[512,256]{1,0:T(8,128)(2,1)S(1)}, bf16[512,256]{1,0:T(8,128)(2,1)S(1)}, u32[]{:S(2)}, u32[]{:S(2)}) collective-permute-start(bf16[512,256]{1,0:T(8,128)(2,1)S(1)} %get-tuple-element.39), channel_id=1, source_target_pairs={{2,0},{4,2},{6,4},{8,6},{10,8},{12,10},{14,12},{16,14},{18,16},{20... | collective-permute-start | bytes 786440 | tf_op jit(solution)/shard_map/ppermute | solution.py:17
  19.5 0.0 copy-done.5
  19.5 0.2 reduce-window.16
  19.7 0.1 convert_reduce_fusion.1
  19.8 0.2 reduce-window.17
  20.0 0.1 convert_reduce_fusion
  20.2 0.0 copy-done.2
  20.2 0.0 collective-permute-done
  20.2 3.4 %collective-permute-done.1 = bf16[512,256]{1,0:T(8,128)(2,1)S(1)} collective-permute-done((bf16[512,256]{1,0:T(8,128)(2,1)S(1)}, bf16[512,256]{1,0:T(8,128)(2,1)S(1)}, u32[]{:S(2)}, u32[]{:S(2)}) %collective-permute-start.1) | collective-permute-done | bytes 262176 | tf_op jit(solution)/shard_map/ppermute | solution.py:17
  23.6 0.1 pad_maximum_fusion
  23.7 0.6 gather_fusion
  24.3 3.4 %convolution_bitcast_fusion.1 = f32[24,128,256]{2,1,0:T(8,128)} fusion(bf16[24,128,256]{2,1,0:T(8,128)(2,1)S(1)} %gather_fusion, pred[24]{0:T(512)(128)(4,1)S(1)} %get-tuple-element.42, bf16[2,24,128,128]{3,2,1,0:T(8,128)(2,1)} %param.15), kind=kOutput, calls=%fused_computation.9 | convolution fusion | flops 202113024 | bytes 5505048 | tf_op jit(solution)/shard_map/tij,tjk->tik/dot_general | solution.py:48
  27.8 0.1 broadcast.112.clone
  27.9 6.1 %scatter_fusion = f32[8,128,256]{2,1,0:T(8,128)S(1)} fusion(f32[8,128,256]{2,1,0:T(8,128)S(1)} %broadcast.112.clone, s32[24]{0:T(128)S(1)} %convert_reduce_fusion.1, f32[24,128,256]{2,1,0:T(8,128)} %convolution_bitcast_fusion.1), kind=kCustom, calls=%fused_computation.4 | custom fusion | flops 786432 | bytes 9437280 | tf_op jit(solution)/shard_map/scatter-add | solution.py:51
  33.9 0.2 multiply_convert_fusion.1
  34.1 1.9 %gather_fusion.1 = bf16[24,128,256]{2,1,0:T(8,128)(2,1)} fusion(bf16[8,128,256]{2,1,0:T(8,128)(2,1)S(1)} %multiply_convert_fusion.1, s32[1024]{0:T(1024)S(1)} %pad_clamp_fusion.2), kind=kCustom, calls=%fused_computation.1.clone | custom fusion | bytes 3145824 | tf_op jit(solution)/shard_map/jit(_take)/gather | solution.py:57
  36.0 4.0 %convolution_bitcast_fusion.3 = f32[24,128,256]{1,2,0:T(8,128)} fusion(bf16[24,128,256]{2,1,0:T(8,128)(2,1)} %gather_fusion.1, pred[24]{0:T(512)(128)(4,1)S(1)} %get-tuple-element.51, bf16[2,24,128,128]{3,2,1,0:T(8,128)(2,1)} %param.15), kind=kOutput, calls=%fused_computation.11 | convolution fusion | flops 202113024 | bytes 5505048 | tf_op jit(solution)/shard_map/tij,tik->tjk/dot_general | solution.py:58
  40.0 3.5 %copy.12 = f32[24,128,256]{2,1,0:T(8,128)} copy(f32[24,128,256]{1,2,0:T(8,128)} %convolution_bitcast_fusion.3) | data formatting | bytes 6291456 | tf_op jit(solution)/shard_map/tij,tik->tjk/dot_general | solution.py:58
  43.5 0.6 gather_fusion.2
  44.2 3.5 %convolution_bitcast_fusion = f32[24,128,256]{2,1,0:T(8,128)} fusion(bf16[24,128,256]{2,1,0:T(8,128)(2,1)S(1)} %gather_fusion.2, pred[24]{0:T(512)(128)(4,1)S(1)} %get-tuple-element.31, bf16[2,24,128,128]{3,2,1,0:T(8,128)(2,1)} %param.15), kind=kOutput, calls=%fused_computation.8 | convolution fusion | flops 202113024 | bytes 5505048 | tf_op jit(solution)/shard_map/tij,tjk->tik/dot_general | solution.py:48
  47.7 0.1 broadcast.112.clone.1
  47.7 6.1 %scatter_fusion.2 = f32[8,128,256]{2,1,0:T(8,128)S(1)} fusion(f32[8,128,256]{2,1,0:T(8,128)S(1)} %broadcast.112.clone.1, s32[24]{0:T(128)S(1)} %convert_reduce_fusion, f32[24,128,256]{2,1,0:T(8,128)} %convolution_bitcast_fusion), kind=kCustom, calls=%fused_computation.6 | custom fusion | flops 786432 | bytes 9437280 | tf_op jit(solution)/shard_map/scatter-add | solution.py:51
  53.8 0.2 multiply_convert_fusion
  54.0 1.8 %gather_fusion.3 = bf16[24,128,256]{2,1,0:T(8,128)(2,1)} fusion(bf16[8,128,256]{2,1,0:T(8,128)(2,1)S(1)} %multiply_convert_fusion, s32[1024]{0:T(1024)S(1)} %pad_clamp_fusion), kind=kCustom, calls=%fused_computation.3.clone | custom fusion | bytes 3145824 | tf_op jit(solution)/shard_map/jit(_take)/gather | solution.py:57
  55.9 2.3 %convolution_bitcast_fusion.2 = f32[24,128,256]{1,2,0:T(8,128)S(1)} fusion(bf16[24,128,256]{2,1,0:T(8,128)(2,1)} %gather_fusion.3, pred[24]{0:T(512)(128)(4,1)S(1)} %get-tuple-element.50, bf16[2,24,128,128]{3,2,1,0:T(8,128)(2,1)} %param.15), kind=kOutput, calls=%fused_computation.10 | convolution fusion | flops 202113024 | bytes 5505048 | tf_op jit(solution)/shard_map/tij,tik->tjk/dot_general | solution.py:58
  58.2 2.4 %copy.14 = f32[24,128,256]{2,1,0:T(8,128)} copy(f32[24,128,256]{1,2,0:T(8,128)S(1)} %convolution_bitcast_fusion.2) | data formatting | bytes 6291456 | tf_op jit(solution)/shard_map/tij,tik->tjk/dot_general | solution.py:58
  60.6 0.2 broadcast_in_dim.34
  60.8 6.1 %scatter_fusion.1 = f32[16,128,256]{2,1,0:T(8,128)S(1)} fusion(f32[16,128,256]{2,1,0:T(8,128)S(1)} %broadcast_in_dim.34, s32[24]{0:T(128)S(1)} %get-tuple-element.47, f32[24,128,256]{2,1,0:T(8,128)} %copy.12), kind=kCustom, calls=%fused_computation.5 | custom fusion | flops 786432 | bytes 9437280 | tf_op jit(solution)/shard_map/scatter-add | solution.py:61
  66.9 6.1 %scatter_fusion.3 = f32[16,128,256]{2,1,0:T(8,128)S(1)} fusion(f32[16,128,256]{2,1,0:T(8,128)S(1)} %scatter_fusion.1, s32[24]{0:T(128)S(1)} %get-tuple-element.46, f32[24,128,256]{2,1,0:T(8,128)} %copy.14), kind=kCustom, calls=%fused_computation.7 | custom fusion | flops 786432 | bytes 9437280 | tf_op jit(solution)/shard_map/scatter-add | solution.py:61
  72.9 0.1 fusion.27
  73.1 6.7 %collective-permute-start.2 = (f32[512,256]{1,0:T(8,128)S(1)}, f32[512,256]{1,0:T(8,128)S(1)}, u32[]{:S(2)}, u32[]{:S(2)}) collective-permute-start(f32[512,256]{1,0:T(8,128)S(1)} %bitcast.50), channel_id=1, source_target_pairs={{0,2},{2,4},{4,6},{6,8},{8,10},{10,12},{12,14},{14,16},{16,18},{18... | collective-permute-start | bytes 1572872 | tf_op jit(solution)/shard_map/ppermute | solution.py:25
  79.8 1.3 %collective-permute-start.3 = (f32[512,256]{1,0:T(8,128)S(1)}, f32[512,256]{1,0:T(8,128)S(1)}, u32[]{:S(2)}, u32[]{:S(2)}) collective-permute-start(f32[512,256]{1,0:T(8,128)S(1)} %bitcast.49), channel_id=1, source_target_pairs={{2,0},{4,2},{6,4},{8,6},{10,8},{12,10},{14,12},{16,14},{18,16},{20... | collective-permute-start | bytes 1572872 | tf_op jit(solution)/shard_map/ppermute | solution.py:25
  81.1 0.1 slice.118
  81.2 0.1 collective-permute-done.2
  81.3 0.1 constant_dynamic-update-slice_fusion
  81.4 0.0 copy-start.1
  81.4 0.0 copy-start.3
  81.4 2.2 %collective-permute-done.3 = f32[512,256]{1,0:T(8,128)S(1)} collective-permute-done((f32[512,256]{1,0:T(8,128)S(1)}, f32[512,256]{1,0:T(8,128)S(1)}, u32[]{:S(2)}, u32[]{:S(2)}) %collective-permute-start.3) | collective-permute-done | bytes 524320 | tf_op jit(solution)/shard_map/ppermute | solution.py:25
  83.6 0.1 fusion.20
  83.7 0.0 copy-start
  83.7 1.0 copy-done
  84.7 0.0 reduce-scatter.2.cloned.1.call-update
  84.7 30.7 %reduce-scatter.2.cloned.1.call-done = f32[1024,128]{1,0:T(8,128)} async-done(((f32[1024,256]{1,0:T(8,128)}), f32[1024,128]{1,0:T(8,128)}) %reduce-scatter.2.cloned.1.call-update) | async-done | bytes 524304 | tf_op jit(solution)/shard_map/reduce_scatter | solution.py:69
  115.5 0.0 copy-done.3
  115.5 2.0 %multiply_add_fusion = f32[1024,128]{1,0:T(8,128)} fusion(f32[1024,128]{1,0:T(8,128)} %reduce-scatter.2.cloned.1.call-done, bf16[1024,128]{1,0:T(8,128)(2,1)S(1)} %copy-done.1, f32[1024]{0:T(1024)S(1)} %copy-done.3), kind=kLoop, calls=%fused_computation.38 | loop fusion | flops 393216 | bytes 1314816 | tf_op jit(solution)/shard_map/add | solution.py:70
  (15 shorter events, 0.1 us)
Async XLA Ops:
  6.5 13.0 %copy-start.5 = (s32[2,1,8]{2,1,0:T(1,128)S(1)}, s32[2,1,8]{2,1,0:T(1,128)}, u32[]{:S(2)}) copy-start(s32[2,1,8]{2,1,0:T(1,128)} %param.16) | copy-start | bytes 196
  6.5 13.6 %copy-start.4 = (s32[2,24]{1,0:T(2,128)S(1)}, s32[2,24]{1,0:T(2,128)}, u32[]{:S(2)}) copy-start(s32[2,24]{1,0:T(2,128)} %param.17) | copy-start | bytes 580
  6.5 13.7 %copy-start.2 = (f32[2,1024]{1,0:T(2,128)S(1)}, f32[2,1024]{1,0:T(2,128)}, u32[]{:S(2)}) copy-start(f32[2,1024]{1,0:T(2,128)} %param.18) | copy-start | bytes 24580
  6.5 108.9 %reduce-scatter.2.cloned.1.call-start = ((), (), s32[]{:S(2)}) async-start(), calls=%async_computation.1 | async-start | bytes 1572864 | tf_op jit(solution)/shard_map/reduce_scatter | solution.py:69
  16.9 3.3 %collective-permute-start = (bf16[512,256]{1,0:T(8,128)(2,1)S(1)}, bf16[512,256]{1,0:T(8,128)(2,1)S(1)}, u32[]{:S(2)}, u32[]{:S(2)}) collective-permute-start(bf16[512,256]{1,0:T(8,128)(2,1)S(1)} %get-tuple-element.38), channel_id=1, source_target_pairs={{0,2},{2,4},{4,6},{6,8},{8,10},{10,12},{12,14},{14,16},{16,18},{18... | collective-permute-start | bytes 786440 | tf_op jit(solution)/shard_map/ppermute | solution.py:16
  18.2 5.4 %collective-permute-start.1 = (bf16[512,256]{1,0:T(8,128)(2,1)S(1)}, bf16[512,256]{1,0:T(8,128)(2,1)S(1)}, u32[]{:S(2)}, u32[]{:S(2)}) collective-permute-start(bf16[512,256]{1,0:T(8,128)(2,1)S(1)} %get-tuple-element.39), channel_id=1, source_target_pairs={{2,0},{4,2},{6,4},{8,6},{10,8},{12,10},{14,12},{16,14},{18,16},{20... | collective-permute-start | bytes 786440 | tf_op jit(solution)/shard_map/ppermute | solution.py:17
  73.1 8.2 %collective-permute-start.2 = (f32[512,256]{1,0:T(8,128)S(1)}, f32[512,256]{1,0:T(8,128)S(1)}, u32[]{:S(2)}, u32[]{:S(2)}) collective-permute-start(f32[512,256]{1,0:T(8,128)S(1)} %bitcast.50), channel_id=1, source_target_pairs={{0,2},{2,4},{4,6},{6,8},{8,10},{10,12},{12,14},{14,16},{16,18},{18... | collective-permute-start | bytes 1572872 | tf_op jit(solution)/shard_map/ppermute | solution.py:25
  79.8 3.8 %collective-permute-start.3 = (f32[512,256]{1,0:T(8,128)S(1)}, f32[512,256]{1,0:T(8,128)S(1)}, u32[]{:S(2)}, u32[]{:S(2)}) collective-permute-start(f32[512,256]{1,0:T(8,128)S(1)} %bitcast.49), channel_id=1, source_target_pairs={{2,0},{4,2},{6,4},{8,6},{10,8},{12,10},{14,12},{16,14},{18,16},{20... | collective-permute-start | bytes 1572872 | tf_op jit(solution)/shard_map/ppermute | solution.py:25
  81.4 34.1 %copy-start.1 = (bf16[1024,128]{1,0:T(8,128)(2,1)S(1)}, bf16[1024,128]{1,0:T(8,128)(2,1)}, u32[]{:S(2)}) copy-start(bf16[1024,128]{1,0:T(8,128)(2,1)} %param.14) | copy-start | bytes 786436
  81.4 34.1 %copy-start.3 = (f32[1024]{0:T(1024)S(1)}, f32[1024]{0:T(1024)}, u32[]{:S(2)}) copy-start(f32[1024]{0:T(1024)} %param.19) | copy-start | bytes 12292
  83.7 1.0 copy-start
Sparse Core Ops, SparseCore 0:
  84.9 30.5 reduce-scatter.1
where the time goes:
time: 125 us; the launch traced here: 124 us
  waiting for transfers between devices  36.4 us (29%)
  other arithmetic  27.6 us (22%)
  between operations  13.7 us (11%)
  matrix products  13.2 us (11%)
  local copies, waits for them, and re-layouts  12.5 us (10%)
  starting transfers between devices  10.6 us (8%)
  blocking collectives  10.3 us (8%)
    reduce_scatter x1, waiting for transfers between devices, local(): curvature = lax.psum_scatter(mine, 'tm', scatter_dimension=1, tiled=True)  30.7 us
    scatter-add x2, other arithmetic, local(): accum = accum.at[local_col].add(back)  12.2 us
    scatter-add x2, other arithmetic, local(): jax.ops.segment_sum(products, tile_row, num_segments=row_blocks, indices_...  12.1 us
    all_gather x1, blocking collectives, local(): full_columns = lax.all_gather(sketch, 'tm', axis=1, tiled=True)  10.3 us
    ppermute x2, starting transfers between devices, from_behind(): return lax.ppermute(shard, axis, pairs)  8.02 us
    dot_general x2, matrix products, local(): jnp.einsum('tij,tjk->tik', tiles[window], picked, preferred_element_type=...  6.93 us
    dot_general x2, matrix products, local(): jnp.einsum('tij,tik->tjk', tiles[window], tile_inputs, preferred_element_...  6.28 us
    dot_general x2, local copies, waits for them, and re-layouts, local(): jnp.einsum('tij,tik->tjk', tiles[window], tile_inputs, preferred_element_...  5.95 us
  transfers between devices with their start and end apart: 5, of which 4 were waited for; matrix products, arithmetic and copies ran while one was open for 1% of the time, Pallas kernels for 0%

commit v1 on v0

v1 whole, which is shorter than its diff:
```python
import functools

import jax
import jax.numpy as jnp
from jax import lax
from jax.experimental import pallas as pl
from jax.experimental.pallas import tpu as pltpu
from jax.sharding import PartitionSpec as P

HB = 4
MAXT = 6
MESH = pl.DeviceIdType.MESH


def kernel(
    n_cell, n_tm,
    counts_ref, cols_ref, sketch_ref, tiles_ref, precision_ref, out_ref,
    blocks, tiles_in, tiles_tr, levels, weighted, terms, edge_out, edge_in, own, parts,
    starts, tile_rows, earlier, latest,
    load_sem, x_send, x_recv, h_send, h_recv, e_send, e_recv, r_send, r_recv,
):
    windows, per_device = cols_ref.shape
    row_blocks = counts_ref.shape[-1]
    owned, size, width = sketch_ref.shape
    spread = owned + 2 * HB
    total = windows * per_device
    d, t = lax.axis_index("cell"), lax.axis_index("tm")
    first_block = d * owned - HB
    lower, upper = d > 0, d < n_cell - 1
    exists = (lower, upper)
    sides = (jnp.maximum(d - 1, 0), jnp.minimum(d + 1, n_cell - 1))
    peers = [lax.rem(t + o, n_tm) for o in range(1, n_tm)]
    senders = [lax.rem(t + n_tm - o, n_tm) for o in range(n_tm)]

    loads = [
        pltpu.make_async_copy(
            tiles_ref.at[pl.ds(w * per_device, per_device)],
            tiles_in.at[pl.ds(w * per_device, per_device)],
            load_sem.at[w],
        )
        for w in range(windows)
    ]
    loads.append(
        pltpu.make_async_copy(sketch_ref, blocks.at[t, pl.ds(HB, owned)], load_sem.at[windows])
    )
    for copy in loads:
        copy.start()

    barrier = pltpu.get_barrier_semaphore()
    for peer in peers:
        pl.semaphore_signal(barrier, inc=1, device_id=(d, peer), device_id_type=MESH)
    for h in range(2):
        @pl.when(exists[h])
        def _():
            pl.semaphore_signal(barrier, inc=1, device_id=(sides[h], t), device_id_type=MESH)
    waits = n_tm - 1 + lower.astype(jnp.int32) + upper.astype(jnp.int32)
    pl.semaphore_wait(barrier, waits)

    def x_copy(o, h):
        piece = pl.ds(h * (owned // 2), owned // 2)
        landing = pl.ds(HB + h * (owned // 2), owned // 2)
        return pltpu.make_async_remote_copy(
            src_ref=sketch_ref.at[piece],
            dst_ref=blocks.at[t, landing],
            send_sem=x_send.at[o - 1, h],
            recv_sem=x_recv.at[o - 1, h],
            device_id=(d, peers[o - 1]),
            device_id_type=MESH,
        )

    def x_arrival(o, h):
        landing = blocks.at[senders[o], pl.ds(HB + h * (owned // 2), owned // 2)]
        return pltpu.make_async_remote_copy(
            src_ref=landing, dst_ref=landing,
            send_sem=x_send.at[o - 1, h], recv_sem=x_recv.at[o - 1, h],
            device_id=(d, peers[o - 1]), device_id_type=MESH,
        )

    def h_copy(o, h):
        slot = senders[o]
        landing = blocks.at[slot, pl.ds((1 - h) * (spread - HB), HB)]
        if o == 0:
            source = sketch_ref.at[pl.ds(h * (owned - HB), HB)]
        else:
            source = blocks.at[slot, pl.ds(HB + h * (owned - HB), HB)]
        return pltpu.make_async_remote_copy(
            src_ref=source, dst_ref=landing,
            send_sem=h_send.at[o, h], recv_sem=h_recv.at[o, 1 - h],
            device_id=(sides[h], t), device_id_type=MESH,
        )

    def h_arrival(o, h):
        landing = blocks.at[senders[o], pl.ds(h * (spread - HB), HB)]
        return pltpu.make_async_remote_copy(
            src_ref=landing, dst_ref=landing,
            send_sem=h_send.at[o, h], recv_sem=h_recv.at[o, h],
            device_id=(sides[h], t), device_id_type=MESH,
        )

    for o in range(1, n_tm):
        for h in range(2):
            x_copy(o, h).start()
    for h in range(2):
        @pl.when(exists[h])
        def _():
            h_copy(0, h).start()

        @pl.when(jnp.logical_not(exists[h]))
        def _():
            for s in range(n_tm):
                blocks[s, pl.ds(h * (spread - HB), HB)] = jnp.zeros((HB, size, width), blocks.dtype)

    for w in range(windows):
        start = jnp.int32(0)
        ends = []
        for b in range(row_blocks):
            starts[w * row_blocks + b] = start
            start = start + counts_ref[w, 0, b]
            ends.append(start)

        def row_of(k, carry, w=w, ends=ends):
            row = jnp.int32(w * row_blocks)
            for b in range(row_blocks - 1):
                row = row + (k >= ends[b]).astype(jnp.int32)
            tile_rows[w * per_device + k] = row
            return carry

        lax.fori_loop(0, per_device, row_of, 0)

    last = tuple(jnp.int32(total) for _ in range(spread))
    for w in range(windows):
        def link(k, last, w=w):
            col = cols_ref[w, k] - first_block
            before = jnp.int32(total)
            for p in range(spread):
                before = jnp.where(col == p, last[p], before)
            earlier[w * per_device + k] = before
            return tuple(
                jnp.where(col == p, w * per_device + k, last[p]) for p in range(spread)
            )

        last = lax.fori_loop(0, per_device, link, last)
    for p in range(spread):
        latest[p] = last[p]

    terms[total] = jnp.zeros(terms.shape[1:], terms.dtype)

    def turn(k, carry):
        tiles_tr[k] = tiles_in[k].T
        return carry

    for w in range(windows):
        for b in range(row_blocks):
            level = precision_ref[w:w + 1, b * size:(b + 1) * size]
            levels[w * row_blocks + b] = jnp.broadcast_to(level, (size, size)).T

    loads[0].wait()
    lax.fori_loop(0, per_device, turn, 0)
    loads[windows].wait()
    for o in range(1, n_tm):
        for h in range(2):
            x_arrival(o, h).wait_recv()

            @pl.when(exists[h])
            def _():
                h_copy(o, h).start()

    for w in range(1, windows):
        loads[w].wait()
        lax.fori_loop(w * per_device, (w + 1) * per_device, turn, 0)
    for h in range(2):
        @pl.when(exists[h])
        def _():
            for o in range(n_tm):
                h_arrival(o, h).wait_recv()

    def forward(i, carry):
        w, b = i // row_blocks, i % row_blocks
        start, count = starts[i], counts_ref[w, 0, b]
        lhs, rhs = [], []
        for j in range(MAXT):
            k = jnp.minimum(start + j, per_device - 1)
            col = jnp.clip(cols_ref[w, k] - first_block, 0, spread - 1)
            tile = tiles_in[w * per_device + k]
            lhs.append(jnp.where(j < count, tile, jnp.zeros_like(tile)))
            rhs.append(jnp.concatenate([blocks[s, col] for s in range(n_tm)], axis=-1))
        product = jnp.dot(
            jnp.concatenate(lhs, axis=1), jnp.concatenate(rhs, axis=0),
            preferred_element_type=jnp.float32,
        )
        level = jnp.concatenate([levels[i]] * (width * n_tm // size), axis=1)
        weighted[i] = (level * product).astype(weighted.dtype)
        return carry

    lax.fori_loop(0, windows * row_blocks, forward, 0)

    unroll = 4

    def backward(i, carry):
        for u in range(unroll):
            k = i * unroll + u
            product = jnp.dot(
                tiles_tr[k], weighted[tile_rows[k]], preferred_element_type=jnp.float32
            )
            terms[k] = product + terms[earlier[k]]
        return carry

    lax.fori_loop(0, total // unroll, backward, 0)

    def e_copy(h):
        return pltpu.make_async_remote_copy(
            src_ref=edge_out.at[h], dst_ref=edge_in.at[1 - h],
            send_sem=e_send.at[h], recv_sem=e_recv.at[1 - h],
            device_id=(sides[h], t), device_id_type=MESH,
        )

    for h in range(2):
        @pl.when(exists[h])
        def _():
            for p in range(HB):
                value = terms[latest[h * (spread - HB) + p]]
                for s in range(n_tm):
                    edge_out[h, s, p] = value[:, s * width:(s + 1) * width]
            e_copy(h).start()

        @pl.when(jnp.logical_not(exists[h]))
        def _():
            edge_in[h] = jnp.zeros(edge_in.shape[1:], edge_in.dtype)

    for h in range(2):
        for p in range(owned // 2):
            value = terms[latest[HB + h * (owned // 2) + p]]
            for s in range(n_tm):
                own[h, s, p] = value[:, s * width:(s + 1) * width]

    def r_copy(o, h):
        return pltpu.make_async_remote_copy(
            src_ref=own.at[h, peers[o - 1]], dst_ref=parts.at[h, o - 1],
            send_sem=r_send.at[h, o - 1], recv_sem=r_recv.at[h, o - 1],
            device_id=(d, peers[o - 1]), device_id_type=MESH,
        )

    near = 1 - lax.rem(d, 2)
    order = (near, 1 - near)
    half = owned // 2

    def has(h):
        return jnp.where(h == 0, lower, upper)

    for h in order:
        @pl.when(has(h))
        def _():
            side = jnp.where(h == 0, sides[0], sides[1])
            pltpu.make_async_remote_copy(
                src_ref=edge_in.at[h], dst_ref=edge_in.at[h],
                send_sem=e_send.at[h], recv_sem=e_recv.at[h],
                device_id=(side, t), device_id_type=MESH,
            ).wait_recv()
        for o in range(1, n_tm):
            peer = peers[o - 1]
            for p in range(half):
                own[h, peer, p] = own[h, peer, p] + edge_in[h, peer, p]
            r_copy(o, h).start()
        for p in range(half):
            own[h, t, p] = own[h, t, p] + edge_in[h, t, p]

    for h in order:
        for o in range(1, n_tm):
            r_copy(o, h).wait_recv()
        for p in range(half):
            value = own[h, t, p]
            for o in range(1, n_tm):
                value = value + parts[h, o - 1, p]
            out_ref[h * half + p] = value

    for h in range(2):
        for o in range(1, n_tm):
            x_copy(o, h).wait_send()
            r_copy(o, h).wait_send()

        @pl.when(exists[h])
        def _():
            for o in range(n_tm):
                h_copy(o, h).wait_send()
            e_copy(h).wait_send()


def local(n_cell, n_tm, sketch, tiles, row_counts, col_index, precision, prior):
    windows, per_device, size, _ = tiles.shape
    rows, width = sketch.shape
    owned = rows // size
    row_blocks = row_counts.shape[-1]
    spread = owned + 2 * HB
    half = owned // 2
    total = windows * per_device
    columns = width * n_tm
    f32, bf16 = jnp.float32, jnp.bfloat16
    vmem, dma = pltpu.VMEM, pltpu.SemaphoreType.DMA
    curvature = pl.pallas_call(
        functools.partial(kernel, n_cell, n_tm),
        out_shape=jax.ShapeDtypeStruct((owned, size, width), f32),
        in_specs=[
            pl.BlockSpec(memory_space=pltpu.SMEM),
            pl.BlockSpec(memory_space=pltpu.SMEM),
            pl.BlockSpec(memory_space=pl.ANY),
            pl.BlockSpec(memory_space=pl.ANY),
            pl.BlockSpec(memory_space=pltpu.VMEM),
        ],
        out_specs=pl.BlockSpec(memory_space=pltpu.VMEM),
        scratch_shapes=[
            vmem((n_tm, spread, size, width), bf16),
            vmem((total, size, size), bf16),
            vmem((total, size, size), bf16),
            vmem((windows * row_blocks, size, size), f32),
            vmem((windows * row_blocks, size, columns), bf16),
            vmem((total + 1, size, columns), f32),
            vmem((2, n_tm, HB, size, width), f32),
            vmem((2, n_tm, HB, size, width), f32),
            vmem((2, n_tm, half, size, width), f32),
            vmem((2, max(n_tm - 1, 1), half, size, width), f32),
            pltpu.SMEM((windows * row_blocks,), jnp.int32),
            pltpu.SMEM((total,), jnp.int32),
            pltpu.SMEM((total,), jnp.int32),
            pltpu.SMEM((spread,), jnp.int32),
            dma((windows + 1,)),
            dma((n_tm, 2)),
            dma((n_tm, 2)),
            dma((n_tm, 2)),
            dma((n_tm, 2)),
            dma((2,)),
            dma((2,)),
            dma((2, n_tm)),
            dma((2, n_tm)),
        ],
        compiler_params=pltpu.CompilerParams(
            collective_id=0, has_side_effects=True, vmem_limit_bytes=48 * 2**20
        ),
        cost_estimate=pl.CostEstimate(
            flops=6 * total * size * size * columns,
            bytes_accessed=total * size * size * 2 + rows * width * 6,
            transcendentals=0,
        ),
    )(
        row_counts, col_index, sketch.reshape(owned, size, width),
        tiles.reshape(total, size, size), precision,
    )
    return prior[:, None] * sketch.astype(f32) + curvature.reshape(rows, width)


def solution(mesh):
    in_specs = (
        P("cell", "tm"),
        P("tm", "cell", None, None),
        P("tm", "cell", None),
        P("tm", "cell"),
        P("tm", "cell"),
        P("cell"),
    )
    out_specs = P("cell", "tm")
    body = functools.partial(local, mesh.shape["cell"], mesh.shape["tm"])
    return jax.shard_map(body, mesh=mesh, in_specs=in_specs, out_specs=out_specs, check_vma=False)
```

time: 125 us -> 43.9 us (0.35)
  the two profiles are of different devices: /device:TPU:0 before, /device:TPU:20 now
where the time goes in v1:
time: 43.9 us; the launch traced here: 43.6 us
  Pallas kernels  38.2 us (87%)
  local copies, waits for them, and re-layouts  4.41 us (10%)
  other arithmetic  1.01 us (2%)
    pallas_call x1, Pallas kernels, local(): pl.pallas_call(functools.partial(kernel, n_cell, n_tm), out_shape=jax.Sha...  38.2 us
    unnamed x12, local copies, waits for them, and re-layouts  4.41 us
    add x1, other arithmetic, local(): return prior[:, None] * sketch.astype(f32) + curvature.reshape(rows, width)  1.01 us

profile of v1, /device:TPU:20, one launch (start us, length us, event | category | flops | bytes accessed | tf_op | source)
XLA Modules:
  0.0 43.6 jit_solution(6623035014053068778)
XLA Ops:
  0.0 0.0 copy-start
  0.0 0.9 %copy-done = bf16[1024,128]{1,0:T(8,128)(2,1)S(1)} copy-done((bf16[1024,128]{1,0:T(8,128)(2,1)S(1)}, bf16[1024,128]{1,0:T(8,128)(2,1)}, u32[]{:S(2)}) %copy-start) | copy-done | bytes 262168
  1.0 0.0 copy-start.1
  1.0 1.4 %copy-done.1 = bf16[2,24,128,128]{3,2,1,0:T(8,128)(2,1)S(1)} copy-done((bf16[2,24,128,128]{3,2,1,0:T(8,128)(2,1)S(1)}, bf16[2,24,128,128]{3,2,1,0:T(8,128)(2,1)}, u32[]{:S(2)}) %copy-start.1) | copy-done | bytes 1572888
  2.4 0.0 copy-start.2
  2.4 0.7 %copy-done.2 = f32[2,1024]{1,0:T(2,128)S(1)} copy-done((f32[2,1024]{1,0:T(2,128)S(1)}, f32[2,1024]{1,0:T(2,128)}, u32[]{:S(2)}) %copy-start.2) | copy-done | bytes 8216
  3.1 0.0 copy-start.3
  3.1 0.7 %copy-done.3 = s32[2,1,8]{2,1,0:T(1,128)S(1)} copy-done((s32[2,1,8]{2,1,0:T(1,128)S(1)}, s32[2,1,8]{2,1,0:T(1,128)}, u32[]{:S(2)}) %copy-start.3) | copy-done | bytes 88
  3.7 0.0 copy-start.4
  3.7 0.7 %copy-done.4 = s32[2,24]{1,0:T(2,128)S(1)} copy-done((s32[2,24]{1,0:T(2,128)S(1)}, s32[2,24]{1,0:T(2,128)}, u32[]{:S(2)}) %copy-start.4) | copy-done | bytes 216
  4.4 0.0 copy-start.5
  4.4 38.2 %shard_map.64 = f32[8,128,128]{2,1,0:T(8,128)S(1)} custom-call(s32[2,1,8]{2,1,0:T(1,128)S(1)} %copy-done.3, s32[2,24]{1,0:T(2,128)S(1)} %copy-done.4, bf16[8,128,128]{2,1,0:T(8,128)(2,1)S(1)} %bitcast.4, bf16[48,128,128]{2,1,0:T(8,128)(2,1)S(1)} %bitcast.5, f32[2,1024]{1,0:T(2,128)S(1)} %copy-done.2), custom_call_target="tpu_custom_call" | custom-call | flops 1207959552 | bytes 2359296 | tf_op jit(solution)/shard_map/pallas_call | solution.py:299
  42.6 0.0 copy-done.5
  42.6 1.0 %bitcast_add_fusion = f32[1024,128]{1,0:T(8,128)} fusion(f32[8,128,128]{2,1,0:T(8,128)S(1)} %shard_map.64, bf16[1024,128]{1,0:T(8,128)(2,1)S(1)} %copy-done, f32[1024]{0:T(1024)S(1)} %copy-done.5), kind=kLoop, calls=%fused_computation | loop fusion | flops 393216 | bytes 1314816 | tf_op jit(solution)/shard_map/add | solution.py:347
Async XLA Ops:
  0.0 0.9 %copy-start = (bf16[1024,128]{1,0:T(8,128)(2,1)S(1)}, bf16[1024,128]{1,0:T(8,128)(2,1)}, u32[]{:S(2)}) copy-start(bf16[1024,128]{1,0:T(8,128)(2,1)} %param.6) | copy-start | bytes 786436
  1.0 1.4 %copy-start.1 = (bf16[2,24,128,128]{3,2,1,0:T(8,128)(2,1)S(1)}, bf16[2,24,128,128]{3,2,1,0:T(8,128)(2,1)}, u32[]{:S(2)}) copy-start(bf16[2,24,128,128]{3,2,1,0:T(8,128)(2,1)} %param.7) | copy-start | bytes 4718596
  2.4 0.7 %copy-start.2 = (f32[2,1024]{1,0:T(2,128)S(1)}, f32[2,1024]{1,0:T(2,128)}, u32[]{:S(2)}) copy-start(f32[2,1024]{1,0:T(2,128)} %precision_ref.1) | copy-start | bytes 24580
  3.1 0.7 %copy-start.3 = (s32[2,1,8]{2,1,0:T(1,128)S(1)}, s32[2,1,8]{2,1,0:T(1,128)}, u32[]{:S(2)}) copy-start(s32[2,1,8]{2,1,0:T(1,128)} %counts_ref.1) | copy-start | bytes 196
  3.7 0.7 %copy-start.4 = (s32[2,24]{1,0:T(2,128)S(1)}, s32[2,24]{1,0:T(2,128)}, u32[]{:S(2)}) copy-start(s32[2,24]{1,0:T(2,128)} %cols_ref.1) | copy-start | bytes 580
  4.4 38.2 %copy-start.5 = (f32[1024]{0:T(1024)S(1)}, f32[1024]{0:T(1024)}, u32[]{:S(2)}) copy-start(f32[1024]{0:T(1024)} %param.11) | copy-start | bytes 12292

commit v2 on v1

--- a/solution.py
+++ b/solution.py
@@ -14,8 +14,11 @@
 
 def kernel(
     n_cell, n_tm,
-    counts_ref, cols_ref, sketch_ref, tiles_ref, precision_ref, out_ref,
-    blocks, tiles_in, tiles_tr, levels, weighted, terms, edge_out, edge_in, own, parts,
+    counts_hbm, cols_hbm, sketch_ref, tiles_ref, precision_hbm, out_ref,
+    counts_ref, cols_ref, precision_ref,
+    blocks, tiles_in, tiles_tr, levels, weighted, terms, own,
+    edge_out, edge_in, parts_out, parts_in,
+    edge_scale_out, edge_scale_in, parts_scale_out, parts_scale_in,
     starts, tile_rows, earlier, latest,
     load_sem, x_send, x_recv, h_send, h_recv, e_send, e_recv, r_send, r_recv,
 ):
@@ -29,6 +32,15 @@
     lower, upper = d > 0, d < n_cell - 1
     exists = (lower, upper)
     sides = (jnp.maximum(d - 1, 0), jnp.minimum(d + 1, n_cell - 1))
+
+    def has(h):
+        return jnp.logical_or(
+            jnp.logical_and(h == 0, lower), jnp.logical_and(h == 1, upper)
+        )
+
+    def side(h):
+        return jnp.where(h == 0, sides[0], sides[1])
+
     peers = [lax.rem(t + o, n_tm) for o in range(1, n_tm)]
     senders = [lax.rem(t + n_tm - o, n_tm) for o in range(n_tm)]
 
@@ -43,7 +55,13 @@
     loads.append(
         pltpu.make_async_copy(sketch_ref, blocks.at[t, pl.ds(HB, owned)], load_sem.at[windows])
     )
-    for copy in loads:
+    small = [
+        pltpu.make_async_copy(source, target, load_sem.at[windows + 1 + i])
+        for i, (source, target) in enumerate(
+            ((counts_hbm, counts_ref), (cols_hbm, cols_ref), (precision_hbm, precision_ref))
+        )
+    ]
+    for copy in small + loads:
         copy.start()
 
     barrier = pltpu.get_barrier_semaphore()
@@ -86,7 +104,7 @@
         return pltpu.make_async_remote_copy(
             src_ref=source, dst_ref=landing,
             send_sem=h_send.at[o, h], recv_sem=h_recv.at[o, 1 - h],
-            device_id=(sides[h], t), device_id_type=MESH,
+            device_id=(side(h), t), device_id_type=MESH,
         )
 
     def h_arrival(o, h):
@@ -94,21 +112,28 @@
         return pltpu.make_async_remote_copy(
             src_ref=landing, dst_ref=landing,
             send_sem=h_send.at[o, h], recv_sem=h_recv.at[o, h],
-            device_id=(sides[h], t), device_id_type=MESH,
-        )
-
-    for o in range(1, n_tm):
-        for h in range(2):
+            device_id=(side(h), t), device_id_type=MESH,
+        )
+
+    far = lax.rem(d, 2)
+    near = 1 - far
+
+    for h in (far, near):
+        for o in range(1, n_tm):
             x_copy(o, h).start()
+
+        @pl.when(has(h))
+        def _():
+            h_copy(0, h).start()
+
     for h in range(2):
-        @pl.when(exists[h])
-        def _():
-            h_copy(0, h).start()
-
         @pl.when(jnp.logical_not(exists[h]))
         def _():
             for s in range(n_tm):
                 blocks[s, pl.ds(h * (spread - HB), HB)] = jnp.zeros((HB, size, width), blocks.dtype)
+
+    for copy in small:
+        copy.wait()
 
     for w in range(windows):
         start = jnp.int32(0)
@@ -154,18 +179,19 @@
             level = precision_ref[w:w + 1, b * size:(b + 1) * size]
             levels[w * row_blocks + b] = jnp.broadcast_to(level, (size, size)).T
 
-    loads[0].wait()
-    lax.fori_loop(0, per_device, turn, 0)
     loads[windows].wait()
-    for o in range(1, n_tm):
-        for h in range(2):
+    for w, h in enumerate((far, near)):
+        for o in range(1, n_tm):
             x_arrival(o, h).wait_recv()
 
-            @pl.when(exists[h])
+            @pl.when(has(h))
             def _():
                 h_copy(o, h).start()
 
-    for w in range(1, windows):
+        if w < windows:
+            loads[w].wait()
+            lax.fori_loop(w * per_device, (w + 1) * per_device, turn, 0)
+    for w in range(2, windows):
         loads[w].wait()
         lax.fori_loop(w * per_device, (w + 1) * per_device, turn, 0)
     for h in range(2):
@@ -207,82 +233,122 @@
 
     lax.fori_loop(0, total // unroll, backward, 0)
 
-    def e_copy(h):
-        return pltpu.make_async_remote_copy(
-            src_ref=edge_out.at[h], dst_ref=edge_in.at[1 - h],
-            send_sem=e_send.at[h], recv_sem=e_recv.at[1 - h],
-            device_id=(sides[h], t), device_id_type=MESH,
-        )
+    def coded(value):
+        largest = jnp.maximum(jnp.max(jnp.abs(value), axis=0, keepdims=True), 1e-33)
+        code = jnp.round(value * (32000.0 / largest))
+        return code.astype(jnp.int32).astype(jnp.int16), largest * (1.0 / 32000.0)
+
+    def decoded(code, scale):
+        return code.astype(jnp.int32).astype(jnp.float32) * scale
+
+    slots = [t] + peers
+    half = owned // 2
+
+    def e_copies(o, h):
+        return [
+            pltpu.make_async_remote_copy(
+                src_ref=out.at[h, slots[o]], dst_ref=landing.at[1 - h, slots[o]],
+                send_sem=e_send.at[h, o, i], recv_sem=e_recv.at[1 - h, o, i],
+                device_id=(side(h), t), device_id_type=MESH,
+            )
+            for i, (out, landing) in enumerate(
+                ((edge_out, edge_in), (edge_scale_out, edge_scale_in))
+            )
+        ]
+
+    def e_arrivals(o, h):
+        return [
+            pltpu.make_async_remote_copy(
+                src_ref=landing.at[h, slots[o]], dst_ref=landing.at[h, slots[o]],
+                send_sem=e_send.at[h, o, i], recv_sem=e_recv.at[h, o, i],
+                device_id=(side(h), t), device_id_type=MESH,
+            )
+            for i, landing in enumerate((edge_in, edge_scale_in))
+        ]
+
+    def r_copies(o, h):
+        return [
+            pltpu.make_async_remote_copy(
+                src_ref=out.at[h, o - 1], dst_ref=landing.at[h, o - 1],
+                send_sem=r_send.at[h, o - 1, i], recv_sem=r_recv.at[h, o - 1, i],
+                device_id=(d, peers[o - 1]), device_id_type=MESH,
+            )
+            for i, (out, landing) in enumerate(
+                ((parts_out, parts_in), (parts_scale_out, parts_scale_in))
+            )
+        ]
+
+    sequence = list(range(1, n_tm)) + [0]
+    for h in (far, near):
+        @pl.when(has(h))
+        def _():
+            for p in range(HB):
+                code, scale = coded(terms[latest[h * (spread - HB) + p]])
+                for s in range(n_tm):
+                    edge_out[h, s, p] = code[:, s * width:(s + 1) * width]
+                    edge_scale_out[h, s, pl.ds(p, 1)] = scale[:, s * width:(s + 1) * width]
+            for o in sequence:
+                for copy in e_copies(o, h):
+                    copy.start()
+
+        @pl.when(jnp.logical_not(has(h)))
+        def _():
+            edge_in[h] = jnp.zeros(edge_in.shape[1:], edge_in.dtype)
+            edge_scale_in[h] = jnp.zeros(edge_scale_in.shape[1:], edge_scale_in.dtype)
 
     for h in range(2):
-        @pl.when(exists[h])
-        def _():
-            for p in range(HB):
-                value = terms[latest[h * (spread - HB) + p]]
-                for s in range(n_tm):
-                    edge_out[h, s, p] = value[:, s * width:(s + 1) * width]
-            e_copy(h).start()
-
-        @pl.when(jnp.logical_not(exists[h]))
-        def _():
-            edge_in[h] = jnp.zeros(edge_in.shape[1:], edge_in.dtype)
-
-    for h in range(2):
-        for p in range(owned // 2):
-            value = terms[latest[HB + h * (owned // 2) + p]]
+        for p in range(half):
+            value = terms[latest[HB + h * half + p]]
             for s in range(n_tm):
                 own[h, s, p] = value[:, s * width:(s + 1) * width]
 
-    def r_copy(o, h):
-        return pltpu.make_async_remote_copy(
-            src_ref=own.at[h, peers[o - 1]], dst_ref=parts.at[h, o - 1],
-            send_sem=r_send.at[h, o - 1], recv_sem=r_recv.at[h, o - 1],
-            device_id=(d, peers[o - 1]), device_id_type=MESH,
-        )
-
-    near = 1 - lax.rem(d, 2)
-    order = (near, 1 - near)
-    half = owned // 2
-
-    def has(h):
-        return jnp.where(h == 0, lower, upper)
-
-    for h in order:
+    for h in (near, far):
+        for o in range(1, n_tm):
+            @pl.when(has(h))
+            def _():
+                for copy in e_arrivals(o, h):
+                    copy.wait_recv()
+
+            slot = slots[o]
+            for p in range(half):
+                value = own[h, slot, p] + decoded(
+                    edge_in[h, slot, p], edge_scale_in[h, slot, pl.ds(p, 1)]
+                )
+                code, scale = coded(value)
+                parts_out[h, o - 1, p] = code
+                parts_scale_out[h, o - 1, pl.ds(p, 1)] = scale
+            for copy in r_copies(o, h):
+                copy.start()
+
+    for h in (near, far):
         @pl.when(has(h))
         def _():
-            side = jnp.where(h == 0, sides[0], sides[1])
-            pltpu.make_async_remote_copy(
-                src_ref=edge_in.at[h], dst_ref=edge_in.at[h],
-                send_sem=e_send.at[h], recv_sem=e_recv.at[h],
-                device_id=(side, t), device_id_type=MESH,
-            ).wait_recv()
+            for copy in e_arrivals(0, h):
+                copy.wait_recv()
+
         for o in range(1, n_tm):
-            peer = peers[o - 1]
-            for p in range(half):
-                own[h, peer, p] = own[h, peer, p] + edge_in[h, peer, p]
-            r_copy(o, h).start()
+            for copy in r_copies(o, h):
+                copy.wait_recv()
         for p in range(half):
-            own[h, t, p] = own[h, t, p] + edge_in[h, t, p]
-
-    for h in order:
-        for o in range(1, n_tm):
-            r_copy(o, h).wait_recv()
-        for p in range(half):
-            value = own[h, t, p]
+            value = own[h, t, p] + decoded(edge_in[h, t, p], edge_scale_in[h, t, pl.ds(p, 1)])
             for o in range(1, n_tm):
-                value = value + parts[h, o - 1, p]
+                value = value + decoded(
+                    parts_in[h, o - 1, p], parts_scale_in[h, o - 1, pl.ds(p, 1)]
+                )
             out_ref[h * half + p] = value
 
-    for h in range(2):
+    for h in (near, far):
         for o in range(1, n_tm):
             x_copy(o, h).wait_send()
-            r_copy(o, h).wait_send()
-
-        @pl.when(exists[h])
+            for copy in r_copies(o, h):
+                copy.wait_send()
+
+        @pl.when(has(h))
         def _():
             for o in range(n_tm):
                 h_copy(o, h).wait_send()
-            e_copy(h).wait_send()
+                for copy in e_copies(o, h):
+                    copy.wait_send()
 
 
 def local(n_cell, n_tm, sketch, tiles, row_counts, col_index, precision, prior):
@@ -294,46 +360,55 @@
     half = owned // 2
     total = windows * per_device
     columns = width * n_tm
-    f32, bf16 = jnp.float32, jnp.bfloat16
+    others = max(n_tm - 1, 1)
+    f32, bf16, i16 = jnp.float32, jnp.bfloat16, jnp.int16
     vmem, dma = pltpu.VMEM, pltpu.SemaphoreType.DMA
     curvature = pl.pallas_call(
         functools.partial(kernel, n_cell, n_tm),
         out_shape=jax.ShapeDtypeStruct((owned, size, width), f32),
         in_specs=[
-            pl.BlockSpec(memory_space=pltpu.SMEM),
-            pl.BlockSpec(memory_space=pltpu.SMEM),
             pl.BlockSpec(memory_space=pl.ANY),
             pl.BlockSpec(memory_space=pl.ANY),
-            pl.BlockSpec(memory_space=pltpu.VMEM),
+            pl.BlockSpec(memory_space=pl.ANY),
+            pl.BlockSpec(memory_space=pl.ANY),
+            pl.BlockSpec(memory_space=pl.ANY),
         ],
         out_specs=pl.BlockSpec(memory_space=pltpu.VMEM),
         scratch_shapes=[
+            pltpu.SMEM(row_counts.shape, jnp.int32),
+            pltpu.SMEM(col_index.shape, jnp.int32),
+            vmem(precision.shape, f32),
             vmem((n_tm, spread, size, width), bf16),
             vmem((total, size, size), bf16),
             vmem((total, size, size), bf16),
             vmem((windows * row_blocks, size, size), f32),
             vmem((windows * row_blocks, size, columns), bf16),
             vmem((total + 1, size, columns), f32),
-            vmem((2, n_tm, HB, size, width), f32),
-            vmem((2, n_tm, HB, size, width), f32),
             vmem((2, n_tm, half, size, width), f32),
-            vmem((2, max(n_tm - 1, 1), half, size, width), f32),
+            vmem((2, n_tm, HB, size, width), i16),
+            vmem((2, n_tm, HB, size, width), i16),
+            vmem((2, others, half, size, width), i16),
+            vmem((2, others, half, size, width), i16),
+            vmem((2, n_tm, HB, width), f32),
+            vmem((2, n_tm, HB, width), f32),
+            vmem((2, others, half, width), f32),
+            vmem((2, others, half, width), f32),
             pltpu.SMEM((windows * row_blocks,), jnp.int32),
             pltpu.SMEM((total,), jnp.int32),
             pltpu.SMEM((total,), jnp.int32),
             pltpu.SMEM((spread,), jnp.int32),
-            dma((windows + 1,)),
+            dma((windows + 4,)),
             dma((n_tm, 2)),
             dma((n_tm, 2)),
             dma((n_tm, 2)),
             dma((n_tm, 2)),
-            dma((2,)),
-            dma((2,)),
-            dma((2, n_tm)),
-            dma((2, n_tm)),
+            dma((2, n_tm, 2)),
+            dma((2, n_tm, 2)),
+            dma((2, n_tm, 2)),
+            dma((2, n_tm, 2)),
         ],
         compiler_params=pltpu.CompilerParams(
-            collective_id=0, has_side_effects=True, vmem_limit_bytes=48 * 2**20
+            collective_id=0, has_side_effects=True, vmem_limit_bytes=60 * 2**20
         ),
         cost_estimate=pl.CostEstimate(
             flops=6 * total * size * size * columns,

time: 43.9 us -> 31.5 us (0.72)
  the two profiles are of different devices: /device:TPU:20 before, /device:TPU:0 now
where the time goes in v2:
time: 31.5 us; the launch traced here: 31.2 us
  Pallas kernels  29.1 us (92%)
  other arithmetic  2.04 us (6%)
    pallas_call x1, Pallas kernels, local(): pl.pallas_call(functools.partial(kernel, n_cell, n_tm), out_shape=jax.Sha...  29.1 us
    add x1, other arithmetic, local(): return prior[:, None] * sketch.astype(f32) + curvature.reshape(rows, width)  2.04 us

profile of v2, /device:TPU:0, one launch (start us, length us, event | category | flops | bytes accessed | tf_op | source)
XLA Modules:
  0.0 31.2 jit_solution(15369036518583217310)
XLA Ops:
  0.0 0.0 copy-start
  0.0 0.0 copy-start.1
  0.0 29.1 %shard_map.64 = f32[8,128,128]{2,1,0:T(8,128)} custom-call(s32[2,1,8]{2,1,0:T(1,128)} %counts_hbm.1, s32[2,24]{1,0:T(2,128)} %cols_hbm.1, bf16[8,128,128]{2,1,0:T(8,128)(2,1)} %bitcast.4, bf16[48,128,128]{2,1,0:T(8,128)(2,1)} %bitcast.5, f32[2,1024]{1,0:T(2,128)} %precision_hbm.1), custom_call_target="tpu_custom_call" | custom-call | flops 1207959552 | bytes 2359296 | tf_op jit(solution)/shard_map/pallas_call | solution.py:366
  29.1 0.0 copy-done
  29.1 0.0 copy-done.1
  29.1 2.0 %bitcast_add_fusion = f32[1024,128]{1,0:T(8,128)} fusion(f32[8,128,128]{2,1,0:T(8,128)} %shard_map.64, bf16[1024,128]{1,0:T(8,128)(2,1)S(1)} %copy-done, f32[1024]{0:T(1024)S(1)} %copy-done.1), kind=kLoop, calls=%fused_computation | loop fusion | flops 393216 | bytes 1314816 | tf_op jit(solution)/shard_map/add | solution.py:422
Async XLA Ops:
  0.0 29.1 %copy-start = (bf16[1024,128]{1,0:T(8,128)(2,1)S(1)}, bf16[1024,128]{1,0:T(8,128)(2,1)}, u32[]{:S(2)}) copy-start(bf16[1024,128]{1,0:T(8,128)(2,1)} %param.6) | copy-start | bytes 786436
  0.0 29.1 %copy-start.1 = (f32[1024]{0:T(1024)S(1)}, f32[1024]{0:T(1024)}, u32[]{:S(2)}) copy-start(f32[1024]{0:T(1024)} %param.11) | copy-start | bytes 12292

commit v3 on v2

--- a/solution.py
+++ b/solution.py
@@ -1,4 +1,5 @@
 import functools
+import math
 
 import jax
 import jax.numpy as jnp
@@ -16,7 +17,7 @@
     n_cell, n_tm,
     counts_hbm, cols_hbm, sketch_ref, tiles_ref, precision_hbm, out_ref,
     counts_ref, cols_ref, precision_ref,
-    blocks, tiles_in, tiles_tr, levels, weighted, terms, own,
+    my_blocks, blocks, tiles_in, tiles_tr, levels, my_weighted, their_weighted, my_terms, their_terms, own,
     edge_out, edge_in, parts_out, parts_in,
     edge_scale_out, edge_scale_in, parts_scale_out, parts_scale_in,
     starts, tile_rows, earlier, latest,
@@ -53,7 +54,7 @@
         for w in range(windows)
     ]
     loads.append(
-        pltpu.make_async_copy(sketch_ref, blocks.at[t, pl.ds(HB, owned)], load_sem.at[windows])
+        pltpu.make_async_copy(sketch_ref, my_blocks.at[pl.ds(HB, owned)], load_sem.at[windows])
     )
     small = [
         pltpu.make_async_copy(source, target, load_sem.at[windows + 1 + i])
@@ -96,8 +97,10 @@
 
     def h_copy(o, h):
         slot = senders[o]
-        landing = blocks.at[slot, pl.ds((1 - h) * (spread - HB), HB)]
+        margin = pl.ds((1 - h) * (spread - HB), HB)
+        landing = blocks.at[slot, margin]
         if o == 0:
+            landing = my_blocks.at[margin]
             source = sketch_ref.at[pl.ds(h * (owned - HB), HB)]
         else:
             source = blocks.at[slot, pl.ds(HB + h * (owned - HB), HB)]
@@ -108,7 +111,8 @@
         )
 
     def h_arrival(o, h):
-        landing = blocks.at[senders[o], pl.ds(h * (spread - HB), HB)]
+        margin = pl.ds(h * (spread - HB), HB)
+        landing = blocks.at[senders[o], margin] if o else my_blocks.at[margin]
         return pltpu.make_async_remote_copy(
             src_ref=landing, dst_ref=landing,
             send_sem=h_send.at[o, h], recv_sem=h_recv.at[o, h],
@@ -129,6 +133,7 @@
     for h in range(2):
         @pl.when(jnp.logical_not(exists[h]))
         def _():
+            my_blocks[pl.ds(h * (spread - HB), HB)] = jnp.zeros((HB, size, width), blocks.dtype)
             for s in range(n_tm):
                 blocks[s, pl.ds(h * (spread - HB), HB)] = jnp.zeros((HB, size, width), blocks.dtype)
 
@@ -168,70 +173,71 @@
     for p in range(spread):
         latest[p] = last[p]
 
-    terms[total] = jnp.zeros(terms.shape[1:], terms.dtype)
-
-    def turn(k, carry):
-        tiles_tr[k] = tiles_in[k].T
-        return carry
-
     for w in range(windows):
         for b in range(row_blocks):
             level = precision_ref[w:w + 1, b * size:(b + 1) * size]
             levels[w * row_blocks + b] = jnp.broadcast_to(level, (size, size)).T
 
-    loads[windows].wait()
-    for w, h in enumerate((far, near)):
+    def turn(w):
+        step = math.gcd(4, per_device)
+
+        def some(i, carry):
+            for u in range(step):
+                k = w * per_device + i * step + u
+                tiles_tr[k] = tiles_in[k].T
+            return carry
+
+        loads[w].wait()
+        lax.fori_loop(0, per_device // step, some, 0)
+
+    def forward(group, weighted):
+        columns = weighted.shape[-1]
+        step = math.gcd(2, windows * row_blocks)
+
+        def some(n, carry):
+            for u in range(step):
+                i = n * step + u
+                w, b = i // row_blocks, i % row_blocks
+                start, count = starts[i], counts_ref[w, 0, b]
+                lhs, rhs = [], []
+                for j in range(MAXT):
+                    k = jnp.minimum(start + j, per_device - 1)
+                    col = jnp.clip(cols_ref[w, k] - first_block, 0, spread - 1)
+                    tile = tiles_in[w * per_device + k]
+                    lhs.append(jnp.where(j < count, tile, jnp.zeros_like(tile)))
+                    parts = [blocks[slot, col] for slot in group] if group else [my_blocks[col]]
+                    rhs.append(parts[0] if len(parts) == 1 else jnp.concatenate(parts, axis=-1))
+                product = jnp.dot(
+                    jnp.concatenate(lhs, axis=1), jnp.concatenate(rhs, axis=0),
+                    preferred_element_type=jnp.float32,
+                )
+                level = jnp.concatenate([levels[i]] * -(-columns // size), axis=1)[:, :columns]
+                weighted[i] = (level * product).astype(weighted.dtype)
+            return carry
+
+        lax.fori_loop(0, windows * row_blocks // step, some, 0)
+
+    def backward(weighted, terms):
+        step = math.gcd(8, total)
+
+        def some(i, carry):
+            for u in range(step):
+                k = i * step + u
+                product = jnp.dot(
+                    tiles_tr[k], weighted[tile_rows[k]], preferred_element_type=jnp.float32
+                )
+                terms[k] = product + terms[earlier[k]]
+            return carry
+
+        lax.fori_loop(0, total // step, some, 0)
+
+    def pass_on(h):
         for o in range(1, n_tm):
             x_arrival(o, h).wait_recv()
 
             @pl.when(has(h))
             def _():
                 h_copy(o, h).start()
-
-        if w < windows:
-            loads[w].wait()
-            lax.fori_loop(w * per_device, (w + 1) * per_device, turn, 0)
-    for w in range(2, windows):
-        loads[w].wait()
-        lax.fori_loop(w * per_device, (w + 1) * per_device, turn, 0)
-    for h in range(2):
-        @pl.when(exists[h])
-        def _():
-            for o in range(n_tm):
-                h_arrival(o, h).wait_recv()
-
-    def forward(i, carry):
-        w, b = i // row_blocks, i % row_blocks
-        start, count = starts[i], counts_ref[w, 0, b]
-        lhs, rhs = [], []
-        for j in range(MAXT):
-            k = jnp.minimum(start + j, per_device - 1)
-            col = jnp.clip(cols_ref[w, k] - first_block, 0, spread - 1)
-            tile = tiles_in[w * per_device + k]
-            lhs.append(jnp.where(j < count, tile, jnp.zeros_like(tile)))
-            rhs.append(jnp.concatenate([blocks[s, col] for s in range(n_tm)], axis=-1))
-        product = jnp.dot(
-            jnp.concatenate(lhs, axis=1), jnp.concatenate(rhs, axis=0),
-            preferred_element_type=jnp.float32,
-        )
-        level = jnp.concatenate([levels[i]] * (width * n_tm // size), axis=1)
-        weighted[i] = (level * product).astype(weighted.dtype)
-        return carry
-
-    lax.fori_loop(0, windows * row_blocks, forward, 0)
-
-    unroll = 4
-
-    def backward(i, carry):
-        for u in range(unroll):
-            k = i * unroll + u
-            product = jnp.dot(
-                tiles_tr[k], weighted[tile_rows[k]], preferred_element_type=jnp.float32
-            )
-            terms[k] = product + terms[earlier[k]]
-        return carry
-
-    lax.fori_loop(0, total // unroll, backward, 0)
 
     def coded(value):
         largest = jnp.maximum(jnp.max(jnp.abs(value), axis=0, keepdims=True), 1e-33)
@@ -278,29 +284,61 @@
             )
         ]
 
-    sequence = list(range(1, n_tm)) + [0]
-    for h in (far, near):
+    def send_edges(terms, group, h):
         @pl.when(has(h))
         def _():
             for p in range(HB):
                 code, scale = coded(terms[latest[h * (spread - HB) + p]])
-                for s in range(n_tm):
-                    edge_out[h, s, p] = code[:, s * width:(s + 1) * width]
-                    edge_scale_out[h, s, pl.ds(p, 1)] = scale[:, s * width:(s + 1) * width]
-            for o in sequence:
+                for i, o in enumerate(group):
+                    part = slice(i * width, (i + 1) * width)
+                    edge_out[h, slots[o], p] = code[:, part]
+                    edge_scale_out[h, slots[o], pl.ds(p, 1)] = scale[:, part]
+            for o in group:
                 for copy in e_copies(o, h):
                     copy.start()
 
-        @pl.when(jnp.logical_not(has(h)))
+    def keep(terms, group, h):
+        for p in range(half):
+            value = terms[latest[HB + h * half + p]]
+            for i, o in enumerate(group):
+                own[h, slots[o], p] = value[:, i * width:(i + 1) * width]
+
+    mine, theirs = [0], list(range(1, n_tm))
+    my_terms[total] = jnp.zeros(my_terms.shape[1:], my_terms.dtype)
+    their_terms[total] = jnp.zeros(their_terms.shape[1:], their_terms.dtype)
+    for h in range(2):
+        @pl.when(jnp.logical_not(exists[h]))
         def _():
             edge_in[h] = jnp.zeros(edge_in.shape[1:], edge_in.dtype)
             edge_scale_in[h] = jnp.zeros(edge_scale_in.shape[1:], edge_scale_in.dtype)
 
+    loads[windows].wait()
+    turn(0)
+    pass_on(far)
+    for w in range(1, windows):
+        turn(w)
     for h in range(2):
-        for p in range(half):
-            value = terms[latest[HB + h * half + p]]
-            for s in range(n_tm):
-                own[h, s, p] = value[:, s * width:(s + 1) * width]
+        @pl.when(exists[h])
+        def _():
+            h_arrival(0, h).wait_recv()
+    forward([], my_weighted)
+    pass_on(near)
+    backward(my_weighted, my_terms)
+    for h in (far, near):
+        send_edges(my_terms, mine, h)
+
+    for h in range(2):
+        @pl.when(exists[h])
+        def _():
+            for o in theirs:
+                h_arrival(o, h).wait_recv()
+    if theirs:
+        forward(peers, their_weighted)
+        backward(their_weighted, their_terms)
+        for h in (far, near):
+            send_edges(their_terms, theirs, h)
+        for h in (near, far):
+            keep(their_terms, theirs, h)
 
     for h in (near, far):
         for o in range(1, n_tm):
@@ -320,6 +358,8 @@
             for copy in r_copies(o, h):
                 copy.start()
 
+    for h in (near, far):
+        keep(my_terms, mine, h)
     for h in (near, far):
         @pl.when(has(h))
         def _():
@@ -378,12 +418,15 @@
             pltpu.SMEM(row_counts.shape, jnp.int32),
             pltpu.SMEM(col_index.shape, jnp.int32),
             vmem(precision.shape, f32),
+            vmem((spread, size, width), bf16),
             vmem((n_tm, spread, size, width), bf16),
             vmem((total, size, size), bf16),
             vmem((total, size, size), bf16),
             vmem((windows * row_blocks, size, size), f32),
-            vmem((windows * row_blocks, size, columns), bf16),
-            vmem((total + 1, size, columns), f32),
+            vmem((windows * row_blocks, size, width), bf16),
+            vmem((windows * row_blocks, size, others * width), bf16),
+            vmem((total + 1, size, width), f32),
+            vmem((total + 1, size, others * width), f32),
             vmem((2, n_tm, half, size, width), f32),
             vmem((2, n_tm, HB, size, width), i16),
             vmem((2, n_tm, HB, size, width), i16),

time: 31.5 us -> 28.7 us (0.911)
  Pallas kernels: 29.1 us -> 26.4 us
    pallas_call x1, Pallas kernels: 29.1 us -> 26.4 us  [local(): pl.pallas_call(functools.partial(kernel, n_cell, n_tm), out_shape=jax.Sha...]
where the time goes in v3:
time: 28.7 us; the launch traced here: 28.5 us
  Pallas kernels  26.4 us (92%)
  other arithmetic  2.04 us (7%)
    pallas_call x1, Pallas kernels, local(): pl.pallas_call(functools.partial(kernel, n_cell, n_tm), out_shape=jax.Sha...  26.4 us
    add x1, other arithmetic, local(): return prior[:, None] * sketch.astype(f32) + curvature.reshape(rows, width)  2.04 us

profile of v3, /device:TPU:0, one launch (start us, length us, event | category | flops | bytes accessed | tf_op | source)
XLA Modules:
  0.0 28.5 jit_solution(5994141423275950305)
XLA Ops:
  0.0 0.0 copy-start
  0.0 0.0 copy-start.1
  0.0 26.4 %shard_map.64 = f32[8,128,128]{2,1,0:T(8,128)} custom-call(s32[2,1,8]{2,1,0:T(1,128)} %counts_hbm.1, s32[2,24]{1,0:T(2,128)} %cols_hbm.1, bf16[8,128,128]{2,1,0:T(8,128)(2,1)} %bitcast.4, bf16[48,128,128]{2,1,0:T(8,128)(2,1)} %bitcast.5, f32[2,1024]{1,0:T(2,128)} %precision_hbm.1), custom_call_target="tpu_custom_call" | custom-call | flops 1207959552 | bytes 2359296 | tf_op jit(solution)/shard_map/pallas_call | solution.py:406
  26.4 0.0 copy-done
  26.4 0.0 copy-done.1
  26.4 2.0 %bitcast_add_fusion = f32[1024,128]{1,0:T(8,128)} fusion(f32[8,128,128]{2,1,0:T(8,128)} %shard_map.64, bf16[1024,128]{1,0:T(8,128)(2,1)S(1)} %copy-done, f32[1024]{0:T(1024)S(1)} %copy-done.1), kind=kLoop, calls=%fused_computation | loop fusion | flops 393216 | bytes 1314816 | tf_op jit(solution)/shard_map/add | solution.py:465
Async XLA Ops:
  0.0 26.4 %copy-start = (bf16[1024,128]{1,0:T(8,128)(2,1)S(1)}, bf16[1024,128]{1,0:T(8,128)(2,1)}, u32[]{:S(2)}) copy-start(bf16[1024,128]{1,0:T(8,128)(2,1)} %param.6) | copy-start | bytes 786436
  0.0 26.4 %copy-start.1 = (f32[1024]{0:T(1024)S(1)}, f32[1024]{0:T(1024)}, u32[]{:S(2)}) copy-start(f32[1024]{0:T(1024)} %param.11) | copy-start | bytes 12292

commit v4 on v3

--- a/solution.py
+++ b/solution.py
@@ -9,6 +9,7 @@
 from jax.sharding import PartitionSpec as P
 
 HB = 4
+CUTS = 2
 MAXT = 6
 MESH = pl.DeviceIdType.MESH
 
@@ -250,11 +251,15 @@
     slots = [t] + peers
     half = owned // 2
 
-    def e_copies(o, h):
+    def cut(c):
+        return pl.ds(c * (half // CUTS), half // CUTS)
+
+    def e_copies(o, h, c):
         return [
             pltpu.make_async_remote_copy(
-                src_ref=out.at[h, slots[o]], dst_ref=landing.at[1 - h, slots[o]],
-                send_sem=e_send.at[h, o, i], recv_sem=e_recv.at[1 - h, o, i],
+                src_ref=out.at[h, slots[o], cut(c)],
+                dst_ref=landing.at[1 - h, slots[o], cut(c)],
+                send_sem=e_send.at[h, o, i, c], recv_sem=e_recv.at[1 - h, o, i, c],
                 device_id=(side(h), t), device_id_type=MESH,
             )
             for i, (out, landing) in enumerate(
@@ -262,21 +267,22 @@
             )
         ]
 
-    def e_arrivals(o, h):
+    def e_arrivals(o, h, c):
         return [
             pltpu.make_async_remote_copy(
-                src_ref=landing.at[h, slots[o]], dst_ref=landing.at[h, slots[o]],
-                send_sem=e_send.at[h, o, i], recv_sem=e_recv.at[h, o, i],
+                src_ref=landing.at[h, slots[o], cut(c)],
+                dst_ref=landing.at[h, slots[o], cut(c)],
+                send_sem=e_send.at[h, o, i, c], recv_sem=e_recv.at[h, o, i, c],
                 device_id=(side(h), t), device_id_type=MESH,
             )
             for i, landing in enumerate((edge_in, edge_scale_in))
         ]
 
-    def r_copies(o, h):
+    def r_copies(o, h, c):
         return [
             pltpu.make_async_remote_copy(
-                src_ref=out.at[h, o - 1], dst_ref=landing.at[h, o - 1],
-                send_sem=r_send.at[h, o - 1, i], recv_sem=r_recv.at[h, o - 1, i],
+                src_ref=out.at[h, o - 1, cut(c)], dst_ref=landing.at[h, o - 1, cut(c)],
+                send_sem=r_send.at[h, o - 1, i, c], recv_sem=r_recv.at[h, o - 1, i, c],
                 device_id=(d, peers[o - 1]), device_id_type=MESH,
             )
             for i, (out, landing) in enumerate(
@@ -292,10 +298,11 @@
                 for i, o in enumerate(group):
                     part = slice(i * width, (i + 1) * width)
                     edge_out[h, slots[o], p] = code[:, part]
-                    edge_scale_out[h, slots[o], pl.ds(p, 1)] = scale[:, part]
+                    edge_scale_out[h, slots[o], p] = scale[:, part]
             for o in group:
-                for copy in e_copies(o, h):
-                    copy.start()
+                for c in range(CUTS):
+                    for copy in e_copies(o, h, c):
+                        copy.start()
 
     def keep(terms, group, h):
         for p in range(half):
@@ -341,54 +348,63 @@
             keep(their_terms, theirs, h)
 
     for h in (near, far):
-        for o in range(1, n_tm):
-            @pl.when(has(h))
-            def _():
-                for copy in e_arrivals(o, h):
-                    copy.wait_recv()
-
+        for o in theirs:
             slot = slots[o]
-            for p in range(half):
-                value = own[h, slot, p] + decoded(
-                    edge_in[h, slot, p], edge_scale_in[h, slot, pl.ds(p, 1)]
-                )
-                code, scale = coded(value)
-                parts_out[h, o - 1, p] = code
-                parts_scale_out[h, o - 1, pl.ds(p, 1)] = scale
-            for copy in r_copies(o, h):
-                copy.start()
-
-    for h in (near, far):
-        keep(my_terms, mine, h)
+            for c in range(CUTS):
+                @pl.when(has(h))
+                def _():
+                    for copy in e_arrivals(o, h, c):
+                        copy.wait_recv()
+
+                for p in range(c * (half // CUTS), (c + 1) * (half // CUTS)):
+                    value = own[h, slot, p] + decoded(
+                        edge_in[h, slot, p], edge_scale_in[h, slot, p]
+                    )
+                    code, scale = coded(value)
+                    parts_out[h, o - 1, p] = code
+                    parts_scale_out[h, o - 1, p] = scale
+                for copy in r_copies(o, h, c):
+                    copy.start()
+
     for h in (near, far):
         @pl.when(has(h))
         def _():
-            for copy in e_arrivals(0, h):
-                copy.wait_recv()
-
-        for o in range(1, n_tm):
-            for copy in r_copies(o, h):
-                copy.wait_recv()
+            for c in range(CUTS):
+                for copy in e_arrivals(0, h, c):
+                    copy.wait_recv()
+
         for p in range(half):
-            value = own[h, t, p] + decoded(edge_in[h, t, p], edge_scale_in[h, t, pl.ds(p, 1)])
-            for o in range(1, n_tm):
-                value = value + decoded(
-                    parts_in[h, o - 1, p], parts_scale_in[h, o - 1, pl.ds(p, 1)]
-                )
-            out_ref[h * half + p] = value
+            own[h, t, p] = my_terms[latest[HB + h * half + p]] + decoded(
+                edge_in[h, t, p], edge_scale_in[h, t, p]
+            )
 
     for h in (near, far):
-        for o in range(1, n_tm):
+        for c in range(CUTS):
+            for o in theirs:
+                for copy in r_copies(o, h, c):
+                    copy.wait_recv()
+            for p in range(c * (half // CUTS), (c + 1) * (half // CUTS)):
+                value = own[h, t, p]
+                for o in theirs:
+                    value = value + decoded(
+                        parts_in[h, o - 1, p], parts_scale_in[h, o - 1, p]
+                    )
+                out_ref[h * half + p] = value
+
+    for h in (near, far):
+        for o in theirs:
             x_copy(o, h).wait_send()
-            for copy in r_copies(o, h):
-                copy.wait_send()
+            for c in range(CUTS):
+                for copy in r_copies(o, h, c):
+                    copy.wait_send()
 
         @pl.when(has(h))
         def _():
             for o in range(n_tm):
                 h_copy(o, h).wait_send()
-                for copy in e_copies(o, h):
-                    copy.wait_send()
+                for c in range(CUTS):
+                    for copy in e_copies(o, h, c):
+                        copy.wait_send()
 
 
 def local(n_cell, n_tm, sketch, tiles, row_counts, col_index, precision, prior):
@@ -432,10 +448,10 @@
             vmem((2, n_tm, HB, size, width), i16),
             vmem((2, others, half, size, width), i16),
             vmem((2, others, half, size, width), i16),
-            vmem((2, n_tm, HB, width), f32),
-            vmem((2, n_tm, HB, width), f32),
-            vmem((2, others, half, width), f32),
-            vmem((2, others, half, width), f32),
+            vmem((2, n_tm, HB, 1, width), f32),
+            vmem((2, n_tm, HB, 1, width), f32),
+            vmem((2, others, half, 1, width), f32),
+            vmem((2, others, half, 1, width), f32),
             pltpu.SMEM((windows * row_blocks,), jnp.int32),
             pltpu.SMEM((total,), jnp.int32),
             pltpu.SMEM((total,), jnp.int32),
@@ -445,10 +461,10 @@
             dma((n_tm, 2)),
             dma((n_tm, 2)),
             dma((n_tm, 2)),
-            dma((2, n_tm, 2)),
-            dma((2, n_tm, 2)),
-            dma((2, n_tm, 2)),
-            dma((2, n_tm, 2)),
+            dma((2, n_tm, 2, CUTS)),
+            dma((2, n_tm, 2, CUTS)),
+            dma((2, n_tm, 2, CUTS)),
+            dma((2, n_tm, 2, CUTS)),
         ],
         compiler_params=pltpu.CompilerParams(
             collective_id=0, has_side_effects=True, vmem_limit_bytes=60 * 2**20

time: 28.7 us -> 29.4 us (1.024)
  Pallas kernels: 26.4 us -> 27.2 us
    pallas_call x1, Pallas kernels: 26.4 us -> 27.2 us  [local(): pl.pallas_call(functools.partial(kernel, n_cell, n_tm), out_shape=jax.Sha...]
where the time goes in v4:
time: 29.4 us; the launch traced here: 29.2 us
  Pallas kernels  27.2 us (93%)
  other arithmetic  2.04 us (7%)
    pallas_call x1, Pallas kernels, local(): pl.pallas_call(functools.partial(kernel, n_cell, n_tm), out_shape=jax.Sha...  27.2 us
    add x1, other arithmetic, local(): return prior[:, None] * sketch.astype(f32) + curvature.reshape(rows, width)  2.04 us

profile of v4, /device:TPU:0, one launch (start us, length us, event | category | flops | bytes accessed | tf_op | source)
XLA Modules:
  0.0 29.2 jit_solution(10632228923382811735)
XLA Ops:
  0.0 0.0 copy-start
  0.0 0.0 copy-start.1
  0.0 27.2 %shard_map.64 = f32[8,128,128]{2,1,0:T(8,128)} custom-call(s32[2,1,8]{2,1,0:T(1,128)} %counts_hbm.1, s32[2,24]{1,0:T(2,128)} %cols_hbm.1, bf16[8,128,128]{2,1,0:T(8,128)(2,1)} %bitcast.4, bf16[48,128,128]{2,1,0:T(8,128)(2,1)} %bitcast.5, f32[2,1024]{1,0:T(2,128)} %precision_hbm.1), custom_call_target="tpu_custom_call" | custom-call | flops 1207959552 | bytes 2359296 | tf_op jit(solution)/shard_map/pallas_call | solution.py:422
  27.2 0.0 copy-done
  27.2 0.0 copy-done.1
  27.2 2.0 %bitcast_add_fusion = f32[1024,128]{1,0:T(8,128)} fusion(f32[8,128,128]{2,1,0:T(8,128)} %shard_map.64, bf16[1024,128]{1,0:T(8,128)(2,1)S(1)} %copy-done, f32[1024]{0:T(1024)S(1)} %copy-done.1), kind=kLoop, calls=%fused_computation | loop fusion | flops 393216 | bytes 1314816 | tf_op jit(solution)/shard_map/add | solution.py:481
Async XLA Ops:
  0.0 27.2 %copy-start = (bf16[1024,128]{1,0:T(8,128)(2,1)S(1)}, bf16[1024,128]{1,0:T(8,128)(2,1)}, u32[]{:S(2)}) copy-start(bf16[1024,128]{1,0:T(8,128)(2,1)} %param.6) | copy-start | bytes 786436
  0.0 27.2 %copy-start.1 = (f32[1024]{0:T(1024)S(1)}, f32[1024]{0:T(1024)}, u32[]{:S(2)}) copy-start(f32[1024]{0:T(1024)} %param.11) | copy-start | bytes 12292
